TPU v7x, 128 devices: a whole 4x4x4 slice. The times are simulated.
128 devices in a mesh: fsdp: 32 (over y_hi, z, x), tp: 4 (over y_lo, core).
Axes of the slice: x: 4, y: 4 (y_hi: 2, y_lo: 2; y = y_hi * 2 + y_lo), z: 4, core: 2. Of those that a mesh axis runs over, the one named last changes fastest.
Arguments:
- tokens: bfloat16 [16384, 1024], P(('fsdp', 'tp')), may hold values from -6 to 6
- segments: int32 [16384], P('fsdp'), may hold values from 0 to 1, as said below
- mix_gain: bfloat16 [1024], replicated, may hold values from 0.5 to 1.5
- in_weight: bfloat16 [3, 1024, 1024], P(None, 'fsdp', 'tp'), may hold values from -0.1875 to 0.1875
- conv_weight: bfloat16 [3, 1024], replicated, may hold values from -3.5 to 3.5
- out_weight: bfloat16 [1024, 1024], P('tp', 'fsdp'), may hold values from -0.1875 to 0.1875
- ffn_gain: bfloat16 [1024], replicated, may hold values from 0.5 to 1.5
- up_gate_weight: bfloat16 [2, 1024, 4608], P(None, 'fsdp', 'tp'), may hold values from -0.1875 to 0.1875
- down_weight: bfloat16 [4608, 1024], P('tp', 'fsdp'), may hold values from -0.09375 to 0.09375
- cotangent: bfloat16 [16384, 1024], P(('fsdp', 'tp')), may hold values from -24 to 24
Outputs:
- mixed: bfloat16 [16384, 1024], P(('fsdp', 'tp'))
- input_grad: float32 [16384, 1024], P(('fsdp', 'tp'))
- mix_gain_grad: float32 [1024], replicated
- in_weight_grad: float32 [3, 1024, 1024], P(None, 'fsdp', 'tp')
- conv_weight_grad: float32 [3, 1024], replicated
- out_weight_grad: float32 [1024, 1024], P('tp', 'fsdp')
- ffn_gain_grad: float32 [1024], replicated
- up_gate_grad: float32 [2, 1024, 4608], P(None, 'fsdp', 'tp')
- down_grad: float32 [4608, 1024], P('tp', 'fsdp')
Inputs may be any that keep to these rules, and one draw needn't show every extreme that they name: `segments`: tokens form documents in order; each token holds its document's number modulo 2, so the value changes exactly where a document starts. Every document but the last has 200 to 2000 tokens, the last has 2 or more.
All inputs are finite; a program needn't handle non-finite values.
Results may differ from a plain program's by a relative error of at most 0.024.
Values may be sent and summed in bfloat16 or wider, within the bound.
No kernel may reach another device: no remote copies, remote signals or barrier semaphores. Data moves between devices by JAX's collectives and lax.ppermute only.
A program may use at most 128 MiB of HBM per device.

v0:
```python
import jax
import jax.numpy as jnp
from jax import lax
from jax.sharding import PartitionSpec as P

EPSILON = 1e-05


def passed_along(value, axis, by):
    size = lax.axis_size(axis)
    pairs = [(i, i + by) for i in range(size) if 0 <= i + by < size]
    return lax.ppermute(value, axis, pairs)


def norm_parts(values):
    scale = lax.rsqrt(jnp.mean(values * values, axis=-1, keepdims=True) + EPSILON)
    return (scale, values * scale)


def norm_back(grad_out, gain, scale, normed):
    grad_norm = grad_out * gain
    return scale * (grad_norm - normed * jnp.mean(grad_norm * normed, axis=-1, keepdims=True))


def fetch_weights(in_weight, out_weight, up_gate_weight, down_weight):
    return (
        lax.all_gather(in_weight, "fsdp", axis=1, tiled=True),
        lax.all_gather(out_weight, "fsdp", axis=1, tiled=True),
        lax.all_gather(up_gate_weight, "fsdp", axis=1, tiled=True),
        lax.all_gather(down_weight, "fsdp", axis=1, tiled=True),
    )


def local(
    tokens,
    segments,
    mix_gain,
    in_weight,
    conv_weight,
    out_weight,
    ffn_gain,
    up_gate_weight,
    down_weight,
    cotangent,
):
    width = tokens.shape[1]
    chan_dev = in_weight.shape[2]
    tp_index = lax.axis_index("tp")
    in_full, out_full, gate_full, down_full = fetch_weights(
        in_weight, out_weight, up_gate_weight, down_weight
    )
    conv_local = lax.dynamic_slice_in_dim(conv_weight, tp_index * chan_dev, chan_dev, 1).astype(
        jnp.float32
    )
    tok_f32 = tokens.astype(jnp.float32)
    scale_one, normed_one = norm_parts(tok_f32)
    gain_one = mix_gain.astype(jnp.float32)
    mix_rows = lax.all_gather(
        (normed_one * gain_one).astype(jnp.bfloat16), "tp", axis=0, tiled=True
    )
    group_rows = mix_rows.shape[0]
    projected = jnp.einsum(
        "rd,jde->jre", mix_rows, in_full, preferred_element_type=jnp.float32
    ).astype(jnp.bfloat16)
    proj_b = projected[0].astype(jnp.float32)
    proj_c = projected[1].astype(jnp.float32)
    proj_x = projected[2].astype(jnp.float32)
    product = proj_b * proj_x
    parity = (segments % 2).astype(jnp.float32)
    parity_row = jnp.zeros((1, chan_dev), jnp.float32).at[0, :2].set(parity[-2:])
    rim_send = jnp.concatenate([product[-2:], parity_row], axis=0)
    rim_recv = passed_along(rim_send, "fsdp", 1)
    padded = jnp.concatenate([rim_recv[:2], product], axis=0)
    parity_pad = jnp.concatenate([rim_recv[2, :2], parity])
    masks = [
        (parity_pad[2 - offset : 2 - offset + group_rows] == parity).astype(jnp.float32)[:, None]
        for offset in range(3)
    ]
    conv_out = jnp.zeros_like(product)
    for offset in range(3):
        conv_out = (
            conv_out
            + conv_local[2 - offset] * masks[offset] * padded[2 - offset : 2 - offset + group_rows]
        )
    mixer_in = (proj_c * conv_out).astype(jnp.bfloat16)
    out_terms = jnp.dot(mixer_in, out_full, preferred_element_type=jnp.float32)
    mixer_out = lax.psum_scatter(out_terms, "tp", scatter_dimension=0, tiled=True)
    middle = tok_f32 + mixer_out
    scale_two, normed_two = norm_parts(middle)
    gain_two = ffn_gain.astype(jnp.float32)
    ffn_rows = lax.all_gather(
        (normed_two * gain_two).astype(jnp.bfloat16), "tp", axis=0, tiled=True
    )
    gate_up = jnp.einsum("rd,jde->jre", ffn_rows, gate_full, preferred_element_type=jnp.float32)
    hidden = (jax.nn.silu(gate_up[0]) * gate_up[1]).astype(jnp.bfloat16)
    ffn_terms = jnp.dot(hidden, down_full, preferred_element_type=jnp.float32)
    ffn_out = lax.psum_scatter(
        ffn_terms.astype(jnp.bfloat16), "tp", scatter_dimension=0, tiled=True
    ).astype(jnp.float32)
    mixed = (middle + ffn_out).astype(jnp.bfloat16)
    cot_rows = lax.all_gather(cotangent, "tp", axis=0, tiled=True)
    grad_hidden = jnp.einsum("rd,fd->rf", cot_rows, down_full, preferred_element_type=jnp.float32)
    grad_down = jnp.einsum("rf,rd->fd", hidden, cot_rows, preferred_element_type=jnp.float32)
    gate_val = gate_up[0]
    up_val = gate_up[1]
    sigma = jax.nn.sigmoid(gate_val)
    grad_up = grad_hidden * gate_val * sigma
    grad_gate = grad_hidden * up_val * sigma * (1.0 + gate_val * (1.0 - sigma))
    grad_pair = jnp.stack([grad_gate, grad_up]).astype(jnp.bfloat16)
    grad_gate_w = jnp.einsum("rd,jrf->jdf", ffn_rows, grad_pair, preferred_element_type=jnp.float32)
    grad_rows_two = jnp.einsum(
        "jrf,jdf->rd", grad_pair, gate_full, preferred_element_type=jnp.float32
    )
    grad_normed_two = lax.psum_scatter(grad_rows_two, "tp", scatter_dimension=0, tiled=True)
    gain_two_grad = jnp.sum(grad_normed_two * normed_two, axis=0)
    grad_middle = cotangent.astype(jnp.float32) + norm_back(
        grad_normed_two, gain_two, scale_two, normed_two
    )
    grad_mix_rows = lax.all_gather(grad_middle.astype(jnp.bfloat16), "tp", axis=0, tiled=True)
    grad_mixer_in = jnp.einsum(
        "rd,cd->rc", grad_mix_rows, out_full, preferred_element_type=jnp.float32
    )
    grad_out_w = jnp.einsum(
        "rc,rd->cd", mixer_in, grad_mix_rows, preferred_element_type=jnp.float32
    )
    grad_c = grad_mixer_in * conv_out
    grad_conv = grad_mixer_in * proj_c
    grad_padded = jnp.zeros((group_rows + 2, chan_dev), jnp.float32)
    conv_grads = []
    for offset in range(3):
        masked = masks[offset] * grad_conv
        grad_padded = grad_padded.at[2 - offset : 2 - offset + group_rows].add(
            conv_local[2 - offset] * masked
        )
        conv_grads.append(jnp.sum(masked * padded[2 - offset : 2 - offset + group_rows], axis=0))
    conv_grad_local = jnp.stack([conv_grads[2], conv_grads[1], conv_grads[0]])
    rim_back = passed_along(grad_padded[:2], "fsdp", -1)
    grad_product = grad_padded[2:] + jnp.concatenate(
        [jnp.zeros((group_rows - 2, chan_dev), jnp.float32), rim_back], axis=0
    )
    grad_proj = jnp.stack([grad_product * proj_x, grad_c, grad_product * proj_b]).astype(
        jnp.bfloat16
    )
    grad_in_w = jnp.einsum("rd,jre->jde", mix_rows, grad_proj, preferred_element_type=jnp.float32)
    grad_rows_one = jnp.einsum(
        "jre,jde->rd", grad_proj, in_full, preferred_element_type=jnp.float32
    )
    grad_normed_one = lax.psum_scatter(
        grad_rows_one.astype(jnp.bfloat16), "tp", scatter_dimension=0, tiled=True
    ).astype(jnp.float32)
    gain_one_grad = jnp.sum(grad_normed_one * normed_one, axis=0)
    input_grad = grad_middle + norm_back(grad_normed_one, gain_one, scale_one, normed_one)
    in_shard, out_shard, gate_shard, down_shard = (
        lax.psum_scatter(
            grad_in_w.astype(jnp.bfloat16), "fsdp", scatter_dimension=1, tiled=True
        ).astype(jnp.float32),
        lax.psum_scatter(
            grad_out_w.astype(jnp.bfloat16), "fsdp", scatter_dimension=1, tiled=True
        ).astype(jnp.float32),
        lax.psum_scatter(
            grad_gate_w.astype(jnp.bfloat16), "fsdp", scatter_dimension=1, tiled=True
        ).astype(jnp.float32),
        lax.psum_scatter(
            grad_down.astype(jnp.bfloat16), "fsdp", scatter_dimension=1, tiled=True
        ).astype(jnp.float32),
    )
    conv_full = lax.dynamic_update_slice_in_dim(
        jnp.zeros((3, width), jnp.float32), conv_grad_local, tp_index * chan_dev, 1
    )
    gain_one_sum, gain_two_sum, conv_sum = lax.psum(
        (gain_one_grad, gain_two_grad, conv_full), ("fsdp", "tp")
    )
    return (
        mixed,
        input_grad,
        gain_one_sum,
        in_shard,
        conv_sum,
        out_shard,
        gain_two_sum,
        gate_shard,
        down_shard,
    )


def solution(mesh):
    placed = (
        P(("fsdp", "tp"), None),
        P("fsdp"),
        P(),
        P(None, "fsdp", "tp"),
        P(),
        P("tp", "fsdp"),
        P(),
        P(None, "fsdp", "tp"),
        P("tp", "fsdp"),
        P(("fsdp", "tp"), None),
    )
    return jax.shard_map(
        local,
        mesh=mesh,
        in_specs=placed,
        out_specs=(
            P(("fsdp", "tp"), None),
            P(("fsdp", "tp"), None),
            P(),
            P(None, "fsdp", "tp"),
            P(),
            P("tp", "fsdp"),
            P(),
            P(None, "fsdp", "tp"),
            P("tp", "fsdp"),
        ),
        check_vma=False,
    )
```

profile of v0, /device:TPU:0, one launch (start us, length us, event | category | flops | bytes accessed | tf_op | source)
XLA Modules:
  0.0 1273.4 jit_solution(7802862768945766624)
XLA Ops:
  9.0 1.8 fusion.20
  14.3 99.7 %all_gather.26 = bf16[256,1024]{0,1:T(8,128)(2,1)S(1)} all-gather(bf16[256,32]{0,1:T(8,128)(2,1)} %param.23), channel_id=1, replica_groups=mesh['fsdp'=32,'tp'=4] {'fsdp'}, dimensions={1}, use_global_device_ids=true | all-gather | bytes 540672 | tf_op jit(solution)/shard_map/all_gather | solution.py:28
  114.1 2.9 fusion.2
  120.2 1.8 fusion.37
  122.1 31.1 %reduce-scatter.7.cloned.1.call-done = f32[128,1024]{1,0:T(8,128)} async-done(((f32[512,1024]{1,0:T(8,128)}), f32[128,1024]{1,0:T(8,128)}) %reduce-scatter.7.cloned.1.call-update) | async-done | bytes 524304 | tf_op jit(solution)/shard_map/reduce_scatter | solution.py:87
  157.2 19.9 %all-gather.12.cloned.1.call-done = bf16[512,1024]{1,0:T(8,128)(2,1)} async-done(((bf16[128,1024]{1,0:T(8,128)(2,1)}), bf16[512,1024]{1,0:T(8,128)(2,1)}) %all-gather.12.cloned.1.call-update) | async-done | bytes 1048592 | tf_op jit(solution)/shard_map/all_gather | solution.py:91
  177.0 87.8 %all-gather.14.cloned.1.call-done = bf16[2,1024,1152]{2,1,0:T(8,128)(2,1)} async-done(((bf16[2,32,1152]{2,1,0:T(8,128)(2,1)}), bf16[2,1024,1152]{2,1,0:T(8,128)(2,1)}) %all-gather.14.cloned.1.call-update) | async-done | bytes 4718608 | tf_op jit(solution)/shard_map/all_gather | solution.py:29
  264.8 7.5 convolution_bitcast_fusion
  272.3 12.6 all-gather.18.cloned.1.call-done
  284.8 76.4 %all-gather.16.cloned.1.call-done = bf16[1152,1024]{0,1:T(8,128)(2,1)} async-done(((bf16[1152,32]{0,1:T(8,128)(2,1)}), bf16[1152,1024]{0,1:T(8,128)(2,1)}) %all-gather.16.cloned.1.call-update) | async-done | bytes 2359312 | tf_op jit(solution)/shard_map/all_gather | solution.py:30
  361.2 6.8 fusion.4
  369.5 4.0 convolution_bitcast_fusion.1
  373.6 25.1 %reduce-scatter.11.cloned.1.call-done = f32[128,1024]{1,0:T(8,128)} async-done(((f32[512,1024]{1,0:T(8,128)}), f32[128,1024]{1,0:T(8,128)}) %reduce-scatter.11.cloned.1.call-update) | async-done | bytes 524304 | tf_op jit(solution)/shard_map/reduce_scatter | solution.py:114
  400.0 1.9 fusion.39
  402.0 4.6 convolution_convert_fusion.1
  406.8 16.9 %all-gather.20.cloned.1.call-done = bf16[512,1024]{1,0:T(8,128)(2,1)} async-done(((bf16[128,1024]{1,0:T(8,128)(2,1)}), bf16[512,1024]{1,0:T(8,128)(2,1)}) %all-gather.20.cloned.1.call-update) | async-done | bytes 1048592 | tf_op jit(solution)/shard_map/all_gather | solution.py:119
  423.7 2.8 multiply_reduce_fusion.3
  426.7 2.3 convolution_convert_fusion.5
  429.3 2.0 scatter-add.11
  433.0 4.2 collective-permute-done.1
  438.3 2.0 bitcast_convert_fusion
  440.4 4.6 convolution_convert_fusion.3
  445.1 6.0 fusion
  451.1 12.7 copy.26
  463.8 2.3 fusion.1
  466.1 2.6 copy.24
  470.6 184.4 %reduce-scatter.17.cloned.1.call-done = bf16[1152,32]{0,1:T(8,128)(2,1)} async-done(((bf16[1152,1024]{0,1:T(8,128)(2,1)}), bf16[1152,32]{0,1:T(8,128)(2,1)}) %reduce-scatter.17.cloned.1.call-update) | async-done | bytes 73744 | tf_op jit(solution)/shard_map/reduce_scatter | solution.py:163
  656.6 182.6 %reduce-scatter.15.cloned.1.call-done = bf16[256,32]{0,1:T(8,128)(2,1)} async-done(((bf16[256,1024]{0,1:T(8,128)(2,1)}), bf16[256,32]{0,1:T(8,128)(2,1)}) %reduce-scatter.15.cloned.1.call-update) | async-done | bytes 16400 | tf_op jit(solution)/shard_map/reduce_scatter | solution.py:157
  840.5 15.8 %reduce-scatter.13.cloned.1.call-done = bf16[128,1024]{1,0:T(8,128)(2,1)} async-done(((bf16[512,1024]{1,0:T(8,128)(2,1)}), bf16[128,1024]{1,0:T(8,128)(2,1)}) %reduce-scatter.13.cloned.1.call-update) | async-done | bytes 262160 | tf_op jit(solution)/shard_map/reduce_scatter | solution.py:148
  857.6 68.7 %all-reduce.5 = (f32[1024]{0:T(1024)}, f32[3,1024]{1,0:T(4,128)}, f32[1024]{0:T(1024)}) all-reduce(f32[1024]{0:T(1024)S(1)} %get-tuple-element.79, f32[3,1024]{1,0:T(4,128)S(1)} %maximum_dynamic-update-slice_fusion, f32[1024]{0:T(1024)S(1)} %get-tuple-element.77), channel_id=1, replica_groups=mesh['fsdp'=32,'tp'=4] {'fsdp','tp'}, use_global_device_ids=true, to_apply=%region_10.11 | all-reduce | flops 5120 | bytes 40960 | tf_op jit(solution)/shard_map/psum | solution.py:170
  926.3 2.2 fusion.16
  928.5 335.1 %all-reduce.9.cloned.1.call-done = (bf16[3,1024,256]{2,0,1:T(4,128)(2,1)}, bf16[2,1024,1152]{2,0,1:T(2,128)(2,1)}) async-done(((bf16[3,1024,256]{2,0,1:T(4,128)(2,1)}, bf16[2,1024,1152]{2,0,1:T(2,128)(2,1)}), (bf16[3,1024,256]{2,0,1:T(4,128)(2,1)}, bf16[2,1024,1152]{2,0,1:T(2,128)(2,1)})) %all-reduce.9.cloned.1.call-update) | async-done | bytes 6291472
  (103 shorter events, 27.6 us)
Async XLA Ops:
  7.2 106.9 %all-gather.8.cloned.1.call-start = ((), (), s32[]{:S(2)}) async-start(), calls=%async_computation.6 | async-start | bytes 1310720 | tf_op jit(solution)/shard_map/all_gather | solution.py:58
  10.8 103.3 %all-gather.10.cloned.1.call-start = ((), (), s32[]{:S(2)}) async-start(), calls=%async_computation.7 | async-start | bytes 1622016 | tf_op jit(solution)/shard_map/all_gather | solution.py:27
  11.6 141.6 %reduce-scatter.7.cloned.1.call-start = ((), (), s32[]{:S(2)}) async-start(), calls=%async_computation.8 | async-start | bytes 2621440 | tf_op jit(solution)/shard_map/reduce_scatter | solution.py:87
  114.1 6.1 copy-start.4
  117.0 306.7 %copy-start.2 = (bf16[3,512,256]{2,1,0:T(8,128)(2,1)}, bf16[3,512,256]{2,1,0:T(8,128)(2,1)S(1)}, u32[]{:S(2)}) copy-start(bf16[3,512,256]{2,1,0:T(8,128)(2,1)S(1)} %fusion.2) | copy-start | bytes 2359300
  117.1 2.6 collective-permute-start
  120.2 1.9 copy-start.6
  120.2 33.0 %copy-start = (bf16[128,1024]{1,0:T(8,128)(2,1)S(1)}, bf16[128,1024]{1,0:T(8,128)(2,1)}, u32[]{:S(2)}) copy-start(bf16[128,1024]{1,0:T(8,128)(2,1)} %param.18) | copy-start | bytes 786436
  122.0 55.0 %all-gather.12.cloned.1.call-start = ((), (), s32[]{:S(2)}) async-start(), calls=%async_computation.9 | async-start | bytes 1310720 | tf_op jit(solution)/shard_map/all_gather | solution.py:91
  155.2 109.6 %all-gather.14.cloned.1.call-start = ((), (), s32[]{:S(2)}) async-start(), calls=%async_computation.10 | async-start | bytes 4866048 | tf_op jit(solution)/shard_map/all_gather | solution.py:29
  155.8 129.0 %all-gather.18.cloned.1.call-start = ((), (), s32[]{:S(2)}) async-start(), calls=%async_computation.13 | async-start | bytes 1310720 | tf_op jit(solution)/shard_map/all_gather | solution.py:101
  156.4 204.8 %all-gather.16.cloned.1.call-start = ((), (), s32[]{:S(2)}) async-start(), calls=%async_computation.11 | async-start | bytes 2433024 | tf_op jit(solution)/shard_map/all_gather | solution.py:30
  157.1 241.5 %reduce-scatter.11.cloned.1.call-start = ((), (), s32[]{:S(2)}) async-start(), calls=%async_computation.14 | async-start | bytes 2621440 | tf_op jit(solution)/shard_map/reduce_scatter | solution.py:114
  361.2 8.3 copy-start.7
  368.0 1.1 copy-start.13
  368.0 1.5 copy-start.14
  373.5 26.5 %copy-start.3 = (bf16[128,1024]{1,0:T(8,128)(2,1)S(1)}, bf16[128,1024]{1,0:T(8,128)(2,1)}, u32[]{:S(2)}) copy-start(bf16[128,1024]{1,0:T(8,128)(2,1)} %param.27) | copy-start | bytes 786436
  373.5 50.2 %all-gather.20.cloned.1.call-start = ((), (), s32[]{:S(2)}) async-start(), calls=%async_computation.15 | async-start | bytes 1310720 | tf_op jit(solution)/shard_map/all_gather | solution.py:119
  401.9 253.1 %reduce-scatter.17.cloned.1.call-start = ((), (), s32[]{:S(2)}) async-start(), calls=%async_computation.18 | async-start | bytes 2433024 | tf_op jit(solution)/shard_map/reduce_scatter | solution.py:163
  406.6 432.6 %reduce-scatter.15.cloned.1.call-start = ((), (), s32[]{:S(2)}) async-start(), calls=%async_computation.17 | async-start | bytes 540672 | tf_op jit(solution)/shard_map/reduce_scatter | solution.py:157
  423.7 3.0 copy-start.5
  429.0 427.3 %reduce-scatter.13.cloned.1.call-start = ((), (), s32[]{:S(2)}) async-start(), calls=%async_computation.16 | async-start | bytes 1310720 | tf_op jit(solution)/shard_map/reduce_scatter | solution.py:148
  431.3 7.0 copy-start.8
  431.3 7.0 copy-start.11
  431.5 5.6 collective-permute-start.1
  440.4 4.8 copy-start.9
  440.4 485.9 %reduce-scatter.9.cloned.1.call-start = ((), (), s32[]{:S(2)}) async-start(), calls=%async_computation.12 | async-start | bytes 1310720 | tf_op jit(solution)/shard_map/reduce_scatter | solution.py:97
  445.1 818.5 %all-reduce.9.cloned.1.call-start = ((), (), s32[]{:S(2)}) async-start(), calls=%async_computation.19 | async-start | bytes 13631488
  451.1 12.7 copy-start.12
  468.7 0.7 copy-start.10
  468.7 457.6 %copy-start.1 = (f32[128,1024]{1,0:T(8,128)S(1)}, f32[128,1024]{1,0:T(8,128)}, u32[]{:S(2)}) copy-start(f32[128,1024]{1,0:T(8,128)} %reduce-scatter.11.cloned.1.call-done) | copy-start | bytes 1572868
Sparse Core Ops, SparseCore 0:
  10.9 23.1 all-gather.7
  37.1 69.8 all-gather.9
  122.2 30.9 reduce-scatter.6
  155.4 21.6 all-gather.11
  180.4 84.3 all-gather.13
  266.4 18.3 all-gather.17
  288.3 72.8 all-gather.15
  373.6 24.9 reduce-scatter.10
  402.0 21.6 all-gather.19
  428.6 226.3 reduce-scatter.16
  657.9 181.2 reduce-scatter.14
  841.6 14.7 reduce-scatter.12
  858.8 21.1 reduce-scatter.8
  882.6 380.9 all-reduce.8
where the time goes:
time: 1270 us
  waiting for transfers between devices  996 us (78%)
  blocking collectives  168 us (13%)
  matrix products  47.6 us (4%)
  other arithmetic  21.9 us (2%)
  local copies, waits for them, and re-layouts  21.6 us (2%)
  between operations  14.9 us (1%)
    unnamed x15, waiting for transfers between devices  338 us
    reduce_scatter x1, waiting for transfers between devices, local(): lax.psum_scatter(grad_down.astype(jnp.bfloat16), 'fsdp', scatter_dimensio...  184 us
    reduce_scatter x1, waiting for transfers between devices, local(): lax.psum_scatter(grad_out_w.astype(jnp.bfloat16), 'fsdp', scatter_dimensi...  183 us
    all_gather x1, blocking collectives, fetch_weights(): lax.all_gather(out_weight, 'fsdp', axis=1, tiled=True)  99.7 us
    all_gather x1, waiting for transfers between devices, fetch_weights(): lax.all_gather(up_gate_weight, 'fsdp', axis=1, tiled=True)  87.8 us
    all_gather x1, waiting for transfers between devices, fetch_weights(): lax.all_gather(down_weight, 'fsdp', axis=1, tiled=True)  76.4 us
    psum x1, blocking collectives, local(): lax.psum((gain_one_grad, gain_two_grad, conv_full), ('fsdp', 'tp'))  68.7 us
    reduce_scatter x1, waiting for transfers between devices, local(): lax.psum_scatter(out_terms, 'tp', scatter_dimension=0, tiled=True)  31.1 us
  transfers between devices with their start and end apart: 16, of which 13 were waited for; matrix products, arithmetic and copies ran while one was open for 5% of the time, Pallas kernels for 0%

commit v1 on v0

v1 whole, which is shorter than its diff:
```python
import jax
import jax.numpy as jnp
from jax import lax
from jax.sharding import Mesh, PartitionSpec as P

EPSILON = 1e-05
F32 = jnp.float32
BF16 = jnp.bfloat16
FSDP = ("yh", "z", "x")
TP = ("yl", "core")
ALL = FSDP + TP


def dot(lhs, rhs, lhs_dim, rhs_dim):
    return lax.dot_general(
        lhs, rhs, (((lhs_dim,), (rhs_dim,)), ((), ())), preferred_element_type=F32
    )


def shifted(value, axis, by):
    size = lax.axis_size(axis)
    return lax.ppermute(value, axis, [(i, (i + by) % size) for i in range(size)])


def swapped(value, axis):
    return lax.ppermute(value, axis, [(0, 1), (1, 0)])


def norm_parts(values):
    scale = lax.rsqrt(jnp.mean(values * values, axis=-1, keepdims=True) + EPSILON)
    return (scale, values * scale)


def norm_back(grad_out, gain, scale, normed):
    grad_norm = grad_out * gain
    return scale * (grad_norm - normed * jnp.mean(grad_norm * normed, axis=-1, keepdims=True))


def put(block, whole, dim, index):
    return lax.dynamic_update_slice_in_dim(whole, jnp.expand_dims(block, dim), index, dim)


def take(whole, dim, index):
    return lax.dynamic_index_in_dim(whole, index, dim, keepdims=False)


def ring_gather(block, axis, dim):
    me = lax.axis_index(axis)
    shape = block.shape[:dim] + (4,) + block.shape[dim:]
    whole = jnp.zeros(shape, block.dtype)
    whole = put(block, whole, dim, me)
    for by in (1, 3, 2):
        whole = put(shifted(block, axis, by), whole, dim, (me - by) % 4)
    return whole


def ring_scatter(whole, axis, dim):
    me = lax.axis_index(axis)
    total = take(whole, dim, me).astype(F32)
    for by in (1, 3, 2):
        total = total + shifted(take(whole, dim, (me + by) % 4), axis, by).astype(F32)
    return total


def gather_rows(shard):
    rows, columns = shard.shape
    other = swapped(shard, "yh")
    first = lax.axis_index("yh") == 0
    pair = jnp.stack([jnp.where(first, shard, other), jnp.where(first, other, shard)])
    half = rows // 2
    upper, lower = pair[:, :half], pair[:, half:]
    upper = ring_gather(upper, "z", 1)
    lower = ring_gather(lower, "x", 1)
    upper = ring_gather(upper, "x", 2)
    lower = ring_gather(lower, "z", 1)
    return jnp.stack([upper, lower], axis=3).reshape(32 * rows, columns)


def scatter_rows(whole):
    columns = whole.shape[1]
    parts = whole.reshape(2, 4, 4, 2, -1, columns)
    upper, lower = parts[:, :, :, 0], parts[:, :, :, 1]
    upper = ring_scatter(upper, "x", 2).astype(BF16)
    lower = ring_scatter(lower, "z", 1).astype(BF16)
    upper = ring_scatter(upper, "z", 1)
    lower = ring_scatter(lower, "x", 1)
    pair = jnp.concatenate([upper, lower], axis=1)
    me = lax.axis_index("yh")
    return take(pair, 0, me) + swapped(take(pair, 0, 1 - me).astype(BF16), "yh").astype(F32)


def gather_tokens(block):
    core = lax.axis_index("core") == 0
    lane = lax.axis_index("yl") == 0

    def ordered(first, mine, other):
        return [jnp.where(first, mine, other), jnp.where(first, other, mine)]

    far = swapped(block, "yl")
    near = jnp.concatenate(ordered(core, block, swapped(block, "core")))
    beyond = jnp.concatenate(ordered(core, far, swapped(far, "core")))
    return jnp.concatenate(ordered(lane, near, beyond))


def scatter_tokens(terms):
    core = lax.axis_index("core")
    lane = lax.axis_index("yl")
    blocks = terms.reshape(2, 2, -1, terms.shape[1])
    sent = take(blocks, 1, 1 - core).astype(BF16)
    pair = take(blocks, 1, core).astype(F32) + swapped(sent, "core").astype(F32)
    sent = take(pair, 0, 1 - lane).astype(BF16)
    return take(pair, 0, lane) + swapped(sent, "yl").astype(F32)


def sum_everywhere(value):
    value = value + swapped(value, "core")
    value = value + swapped(value, "yl")
    value = value + swapped(value, "yh")
    for axis in ("x", "z"):
        value = (value + shifted(value, axis, 2)) + (
            shifted(value, axis, 1) + shifted(value, axis, 3)
        )
    return value


def along_tokens(value, by):
    pairs = [(i, i + by) for i in range(32) if 0 <= i + by < 32]
    return lax.ppermute(value, FSDP, pairs)


def local(
    tokens,
    segments,
    mix_gain,
    in_weight,
    conv_weight,
    out_weight,
    ffn_gain,
    up_gate_weight,
    down_weight,
    cotangent,
):
    width = tokens.shape[1]
    chan_dev = in_weight.shape[2]
    hidden_dev = up_gate_weight.shape[2]
    shard_rows = in_weight.shape[1]
    tp_index = lax.axis_index("yl") * 2 + lax.axis_index("core")

    in_rows = jnp.concatenate([in_weight[0], in_weight[1], in_weight[2]], axis=1)
    in_full = gather_rows(in_rows)
    mid_rows = jnp.concatenate([out_weight.T, up_gate_weight[0], up_gate_weight[1]], axis=1)
    mid_full = gather_rows(mid_rows)
    out_full = mid_full[:, :chan_dev]
    gate_full = mid_full[:, chan_dev:]
    down_full = gather_rows(down_weight.T)

    conv_local = lax.dynamic_slice_in_dim(conv_weight, tp_index * chan_dev, chan_dev, 1).astype(F32)
    tok_f32 = tokens.astype(F32)
    scale_one, normed_one = norm_parts(tok_f32)
    gain_one = mix_gain.astype(F32)
    mix_rows = gather_tokens((normed_one * gain_one).astype(BF16))
    group_rows = mix_rows.shape[0]
    projected = dot(mix_rows, in_full, 1, 0).astype(BF16)
    proj_b = projected[:, :chan_dev].astype(F32)
    proj_c = projected[:, chan_dev : 2 * chan_dev].astype(F32)
    proj_x = projected[:, 2 * chan_dev :].astype(F32)
    product = proj_b * proj_x
    parity = (segments % 2).astype(F32)
    parity_row = jnp.zeros((1, chan_dev), F32).at[0, :2].set(parity[-2:])
    rim_send = jnp.concatenate([product[-2:], parity_row], axis=0)
    rim_recv = along_tokens(rim_send, 1)
    padded = jnp.concatenate([rim_recv[:2], product], axis=0)
    parity_pad = jnp.concatenate([rim_recv[2, :2], parity])
    masks = [
        (parity_pad[2 - offset : 2 - offset + group_rows] == parity).astype(F32)[:, None]
        for offset in range(3)
    ]
    conv_out = jnp.zeros_like(product)
    for offset in range(3):
        conv_out = (
            conv_out
            + conv_local[2 - offset] * masks[offset] * padded[2 - offset : 2 - offset + group_rows]
        )
    mixer_in = (proj_c * conv_out).astype(BF16)
    middle = tok_f32 + scatter_tokens(dot(mixer_in, out_full, 1, 1))
    scale_two, normed_two = norm_parts(middle)
    gain_two = ffn_gain.astype(F32)
    ffn_rows = gather_tokens((normed_two * gain_two).astype(BF16))
    cot_rows = gather_tokens(cotangent)
    grad_hidden = dot(cot_rows, down_full, 1, 0)
    gate_up = dot(ffn_rows, gate_full, 1, 0)
    gate_val = gate_up[:, :hidden_dev]
    up_val = gate_up[:, hidden_dev:]
    sigma = jax.nn.sigmoid(gate_val)
    hidden = (gate_val * sigma * up_val).astype(BF16)
    grad_up = grad_hidden * gate_val * sigma
    grad_gate = grad_hidden * up_val * sigma * (1.0 + gate_val * (1.0 - sigma))
    grad_pair = jnp.concatenate([grad_gate.astype(BF16), grad_up.astype(BF16)], axis=1)
    grad_normed_two = scatter_tokens(dot(grad_pair, gate_full, 1, 1))
    grad_down = dot(cot_rows, hidden, 0, 0).astype(BF16)
    grad_gate_w = dot(ffn_rows, grad_pair, 0, 0).astype(BF16)
    mixed = (middle + scatter_tokens(dot(hidden, down_full, 1, 1))).astype(BF16)

    gain_two_grad = jnp.sum(grad_normed_two * normed_two, axis=0)
    grad_middle = cotangent.astype(F32) + norm_back(grad_normed_two, gain_two, scale_two, normed_two)
    grad_mix_rows = gather_tokens(grad_middle.astype(BF16))
    grad_mixer_in = dot(grad_mix_rows, out_full, 1, 0)
    grad_out_w = dot(grad_mix_rows, mixer_in, 0, 0).astype(BF16)
    grad_c = grad_mixer_in * conv_out
    grad_conv = grad_mixer_in * proj_c
    grad_padded = jnp.zeros((group_rows + 2, chan_dev), F32)
    conv_grads = []
    for offset in range(3):
        masked = masks[offset] * grad_conv
        grad_padded = grad_padded + jnp.pad(
            conv_local[2 - offset] * masked, ((2 - offset, offset), (0, 0))
        )
        conv_grads.append(jnp.sum(masked * padded[2 - offset : 2 - offset + group_rows], axis=0))
    conv_grad_local = jnp.stack([conv_grads[2], conv_grads[1], conv_grads[0]])
    rim_back = along_tokens(grad_padded[:2], -1)
    grad_product = grad_padded[2:] + jnp.pad(rim_back, ((group_rows - 2, 0), (0, 0)))
    grad_proj = jnp.concatenate(
        [
            (grad_product * proj_x).astype(BF16),
            grad_c.astype(BF16),
            (grad_product * proj_b).astype(BF16),
        ],
        axis=1,
    )
    grad_in_w = dot(mix_rows, grad_proj, 0, 0).astype(BF16)
    grad_normed_one = scatter_tokens(dot(grad_proj, in_full, 1, 1))
    gain_one_grad = jnp.sum(grad_normed_one * normed_one, axis=0)
    input_grad = grad_middle + norm_back(grad_normed_one, gain_one, scale_one, normed_one)

    down_shard = scatter_rows(grad_down)
    gate_shard = scatter_rows(grad_gate_w)
    last_shard = scatter_rows(jnp.concatenate([grad_out_w, grad_in_w], axis=1))
    out_shard = last_shard[:, :chan_dev]
    in_shard = last_shard[:, chan_dev:]

    conv_full = lax.dynamic_update_slice_in_dim(
        jnp.zeros((3, width), F32), conv_grad_local, tp_index * chan_dev, 1
    )
    sums = sum_everywhere(
        jnp.concatenate([gain_one_grad[None], gain_two_grad[None], conv_full], axis=0)
    )
    return (
        mixed,
        input_grad,
        sums[0],
        jnp.stack([in_shard[:, i * chan_dev : (i + 1) * chan_dev] for i in range(3)]),
        sums[2:],
        out_shard.T,
        sums[1],
        jnp.stack([gate_shard[:, :hidden_dev], gate_shard[:, hidden_dev:]]),
        down_shard.T,
    )


def solution(mesh):
    fine = Mesh(mesh.devices.reshape(2, 4, 4, 2, 2), ALL)
    placed = (
        P(ALL, None),
        P(FSDP),
        P(),
        P(None, FSDP, TP),
        P(),
        P(TP, FSDP),
        P(),
        P(None, FSDP, TP),
        P(TP, FSDP),
        P(ALL, None),
    )
    return jax.shard_map(
        local,
        mesh=fine,
        in_specs=placed,
        out_specs=(
            P(ALL, None),
            P(ALL, None),
            P(),
            P(None, FSDP, TP),
            P(),
            P(TP, FSDP),
            P(),
            P(None, FSDP, TP),
            P(TP, FSDP),
        ),
        check_vma=False,
    )
```

time: 1270 us -> 506 us (0.40)
  waiting for transfers between devices: 996 us -> 303 us
  blocking collectives: 168 us -> 0 us
  starting transfers between devices: 3.46 us -> 140 us
  matrix products: 47.6 us -> 18.8 us
    reduce_scatter x6 -> x0, waiting for transfers between devices: 439 us -> none  [the longest x1 184 us: local(): lax.psum_scatter(grad_down.astype(jnp.bfloat16), 'fsdp', scatter_dimensio...]
    unnamed x15 -> x0, waiting for transfers between devices: 338 us -> none
    ppermute x2 -> x109, waiting for transfers between devices: 5.48 us -> 303 us  [the longest x78 238 us: shifted(): lax.ppermute(value, axis, [(i, (i + by) % size) for i in range(size)])]
    all_gather x7 -> x0, waiting for transfers between devices: 213 us -> none  [the longest x1 87.8 us: fetch_weights(): lax.all_gather(up_gate_weight, 'fsdp', axis=1, tiled=True)]
    ppermute x2 -> x109, starting transfers between devices: 2.71 us -> 140 us  [the longest x78 120 us: shifted(): lax.ppermute(value, axis, [(i, (i + by) % size) for i in range(size)])]
    all_gather x1 -> x0, blocking collectives: 99.7 us -> none  [fetch_weights(): lax.all_gather(out_weight, 'fsdp', axis=1, tiled=True)]
    psum x1 -> x0, blocking collectives: 68.7 us -> none  [local(): lax.psum((gain_one_grad, gain_two_grad, conv_full), ('fsdp', 'tp'))]
    dot_general x12, matrix products: 47.6 us -> 18.8 us  [dot(): lax.dot_general(lhs, rhs, (((lhs_dim,), (rhs_dim,)), ((), ())), preferred...]
  transfers between devices with their start and end apart: 16 -> 109, of which waited for: 13 -> 72; matrix products, arithmetic and copies ran while one was open for 5% -> 5% of each run, Pallas kernels for 0% -> 0%
where the time goes in v1:
time: 506 us; the launch traced here: 497 us
  waiting for transfers between devices  303 us (60%)
  starting transfers between devices  140 us (28%)
  other arithmetic  20.6 us (4%)
  matrix products  18.8 us (4%)
  local copies, waits for them, and re-layouts  11.4 us (2%)
    ppermute x78, waiting for transfers between devices, shifted(): lax.ppermute(value, axis, [(i, (i + by) % size) for i in range(size)])  238 us
    ppermute x78, starting transfers between devices, shifted(): lax.ppermute(value, axis, [(i, (i + by) % size) for i in range(size)])  120 us
    ppermute x29, waiting for transfers between devices, swapped(): return lax.ppermute(value, axis, [(0, 1), (1, 0)])  59.2 us
    dot_general x12, matrix products, dot(): lax.dot_general(lhs, rhs, (((lhs_dim,), (rhs_dim,)), ((), ())), preferred...  18.8 us
    ppermute x29, starting transfers between devices, swapped(): return lax.ppermute(value, axis, [(0, 1), (1, 0)])  15.6 us
  transfers between devices with their start and end apart: 109, of which 72 were waited for; matrix products, arithmetic and copies ran while one was open for 5% of the time, Pallas kernels for 0%

profile of v1, /device:TPU:0, one launch (start us, length us, event | category | flops | bytes accessed | tf_op | source)
XLA Modules:
  0.0 496.8 jit_solution(16956886746981141625)
XLA Ops:
  15.3 5.6 %collective-permute-done.3 = bf16[32,768]{1,0:T(8,128)(2,1)S(1)} collective-permute-done((bf16[32,768]{1,0:T(8,128)(2,1)S(1)}, bf16[32,768]{1,0:T(8,128)(2,1)S(1)}, u32[]{:S(2)}, u32[]{:S(2)}) %collective-permute-start.3) | collective-permute-done | bytes 49184 | tf_op jit(solution)/shard_map/ppermute | solution.py:26
  21.6 5.1 %collective-permute-done.35 = bf16[32,1152]{1,0:T(8,128)(2,1)S(1)} collective-permute-done((bf16[32,1152]{1,0:T(8,128)(2,1)S(1)}, bf16[32,1152]{1,0:T(8,128)(2,1)S(1)}, u32[]{:S(2)}, u32[]{:S(2)}) %collective-permute-start.35) | collective-permute-done | bytes 73760 | tf_op jit(solution)/shard_map/ppermute | solution.py:26
  38.0 4.2 collective-permute-done.12
  58.4 5.1 %collective-permute-done.42 = bf16[2,16,1152]{2,1,0:T(8,128)(2,1)S(1)} collective-permute-done((bf16[2,16,1152]{2,1,0:T(8,128)(2,1)S(1)}, bf16[2,16,1152]{2,1,0:T(8,128)(2,1)S(1)}, u32[]{:S(2)}, u32[]{:S(2)}) %collective-permute-start.42) | collective-permute-done | bytes 73760 | tf_op jit(solution)/shard_map/ppermute | solution.py:22
  68.9 4.9 collective-permute-done.44
  74.5 4.8 collective-permute-done.36
  85.2 5.2 %collective-permute-done.38 = bf16[2,16,1152]{2,1,0:T(8,128)(2,1)S(1)} collective-permute-done((bf16[2,16,1152]{2,1,0:T(8,128)(2,1)S(1)}, bf16[2,16,1152]{2,1,0:T(8,128)(2,1)S(1)}, u32[]{:S(2)}, u32[]{:S(2)}) %collective-permute-start.38) | collective-permute-done | bytes 73760 | tf_op jit(solution)/shard_map/ppermute | solution.py:22
  91.1 6.0 %collective-permute-done.17 = bf16[32,2560]{1,0:T(8,128)(2,1)S(1)} collective-permute-done((bf16[32,2560]{1,0:T(8,128)(2,1)S(1)}, bf16[32,2560]{1,0:T(8,128)(2,1)S(1)}, u32[]{:S(2)}, u32[]{:S(2)}) %collective-permute-start.17) | collective-permute-done | bytes 163872 | tf_op jit(solution)/shard_map/ppermute | solution.py:26
  104.3 5.2 %collective-permute-start.8 = (bf16[2,4,16,768]{3,2,1,0:T(8,128)(2,1)S(1)}, bf16[2,4,16,768]{3,2,1,0:T(8,128)(2,1)S(1)}, u32[]{:S(2)}, u32[]{:S(2)}) collective-permute-start(bf16[2,4,16,768]{3,2,1,0:T(8,128)(2,1)S(1)} %bitcast_dynamic-update-slice_fusion.44), channel_id=1, source_target_pairs={{0,12},{4,0},{8,4},{12,8},{1,13},{5,1},{9,5},{13,9},{2,14},{6,2},{... | collective-permute-start | bytes 589832 | tf_op jit(solution)/shard_map/ppermute | solution.py:22
  110.9 5.6 %collective-permute-done.8 = bf16[2,4,16,768]{3,2,1,0:T(8,128)(2,1)S(1)} collective-permute-done((bf16[2,4,16,768]{3,2,1,0:T(8,128)(2,1)S(1)}, bf16[2,4,16,768]{3,2,1,0:T(8,128)(2,1)S(1)}, u32[]{:S(2)}, u32[]{:S(2)}) %collective-permute-start.8) | collective-permute-done | bytes 196640 | tf_op jit(solution)/shard_map/ppermute | solution.py:22
  119.8 6.8 %collective-permute-done.24 = bf16[2,16,2560]{2,1,0:T(8,128)(2,1)S(1)} collective-permute-done((bf16[2,16,2560]{2,1,0:T(8,128)(2,1)S(1)}, bf16[2,16,2560]{2,1,0:T(8,128)(2,1)S(1)}, u32[]{:S(2)}, u32[]{:S(2)}) %collective-permute-start.24) | collective-permute-done | bytes 163872 | tf_op jit(solution)/shard_map/ppermute | solution.py:22
  133.6 5.9 %collective-permute-done.26 = bf16[2,16,2560]{2,1,0:T(8,128)(2,1)S(1)} collective-permute-done((bf16[2,16,2560]{2,1,0:T(8,128)(2,1)S(1)}, bf16[2,16,2560]{2,1,0:T(8,128)(2,1)S(1)}, u32[]{:S(2)}, u32[]{:S(2)}) %collective-permute-start.26) | collective-permute-done | bytes 163872 | tf_op jit(solution)/shard_map/ppermute | solution.py:22
  139.8 6.2 %collective-permute-done.18 = bf16[2,16,2560]{2,1,0:T(8,128)(2,1)S(1)} collective-permute-done((bf16[2,16,2560]{2,1,0:T(8,128)(2,1)S(1)}, bf16[2,16,2560]{2,1,0:T(8,128)(2,1)S(1)}, u32[]{:S(2)}, u32[]{:S(2)}) %collective-permute-start.18) | collective-permute-done | bytes 163872 | tf_op jit(solution)/shard_map/ppermute | solution.py:22
  146.0 5.3 %collective-permute-done.19 = bf16[2,16,2560]{2,1,0:T(8,128)(2,1)S(1)} collective-permute-done((bf16[2,16,2560]{2,1,0:T(8,128)(2,1)S(1)}, bf16[2,16,2560]{2,1,0:T(8,128)(2,1)S(1)}, u32[]{:S(2)}, u32[]{:S(2)}) %collective-permute-start.19) | collective-permute-done | bytes 163872 | tf_op jit(solution)/shard_map/ppermute | solution.py:22
  151.3 6.8 %collective-permute-done.20 = bf16[2,16,2560]{2,1,0:T(8,128)(2,1)S(1)} collective-permute-done((bf16[2,16,2560]{2,1,0:T(8,128)(2,1)S(1)}, bf16[2,16,2560]{2,1,0:T(8,128)(2,1)S(1)}, u32[]{:S(2)}, u32[]{:S(2)}) %collective-permute-start.20) | collective-permute-done | bytes 163872 | tf_op jit(solution)/shard_map/ppermute | solution.py:22
  171.6 4.6 collective-permute-start.27
  176.7 14.1 %collective-permute-done.27 = bf16[2,4,16,2560]{3,2,1,0:T(8,128)(2,1)S(1)} collective-permute-done((bf16[2,4,16,2560]{3,2,1,0:T(8,128)(2,1)S(1)}, bf16[2,4,16,2560]{3,2,1,0:T(8,128)(2,1)S(1)}, u32[]{:S(2)}, u32[]{:S(2)}) %collective-permute-start.27) | collective-permute-done | bytes 655392 | tf_op jit(solution)/shard_map/ppermute | solution.py:22
  192.7 13.6 %collective-permute-done.28 = bf16[2,4,16,2560]{3,2,1,0:T(8,128)(2,1)S(1)} collective-permute-done((bf16[2,4,16,2560]{3,2,1,0:T(8,128)(2,1)S(1)}, bf16[2,4,16,2560]{3,2,1,0:T(8,128)(2,1)S(1)}, u32[]{:S(2)}, u32[]{:S(2)}) %collective-permute-start.28) | collective-permute-done | bytes 655392 | tf_op jit(solution)/shard_map/ppermute | solution.py:22
  209.1 13.3 %collective-permute-done.29 = bf16[2,4,16,2560]{3,2,1,0:T(8,128)(2,1)S(1)} collective-permute-done((bf16[2,4,16,2560]{3,2,1,0:T(8,128)(2,1)S(1)}, bf16[2,4,16,2560]{3,2,1,0:T(8,128)(2,1)S(1)}, u32[]{:S(2)}, u32[]{:S(2)}) %collective-permute-start.29) | collective-permute-done | bytes 655392 | tf_op jit(solution)/shard_map/ppermute | solution.py:22
  223.2 14.2 %collective-permute-done.21 = bf16[2,4,16,2560]{3,2,1,0:T(8,128)(2,1)S(1)} collective-permute-done((bf16[2,4,16,2560]{3,2,1,0:T(8,128)(2,1)S(1)}, bf16[2,4,16,2560]{3,2,1,0:T(8,128)(2,1)S(1)}, u32[]{:S(2)}, u32[]{:S(2)}) %collective-permute-start.21) | collective-permute-done | bytes 655392 | tf_op jit(solution)/shard_map/ppermute | solution.py:22
  237.4 14.2 %collective-permute-done.22 = bf16[2,4,16,2560]{3,2,1,0:T(8,128)(2,1)S(1)} collective-permute-done((bf16[2,4,16,2560]{3,2,1,0:T(8,128)(2,1)S(1)}, bf16[2,4,16,2560]{3,2,1,0:T(8,128)(2,1)S(1)}, u32[]{:S(2)}, u32[]{:S(2)}) %collective-permute-start.22) | collective-permute-done | bytes 655392 | tf_op jit(solution)/shard_map/ppermute | solution.py:22
  251.7 12.0 %collective-permute-done.23 = bf16[2,4,16,2560]{3,2,1,0:T(8,128)(2,1)S(1)} collective-permute-done((bf16[2,4,16,2560]{3,2,1,0:T(8,128)(2,1)S(1)}, bf16[2,4,16,2560]{3,2,1,0:T(8,128)(2,1)S(1)}, u32[]{:S(2)}, u32[]{:S(2)}) %collective-permute-start.23) | collective-permute-done | bytes 655392 | tf_op jit(solution)/shard_map/ppermute | solution.py:22
  267.2 8.3 %collective-permute-done.31 = bf16[128,1024]{1,0:T(8,128)(2,1)S(1)} collective-permute-done((bf16[128,1024]{1,0:T(8,128)(2,1)S(1)}, bf16[128,1024]{1,0:T(8,128)(2,1)S(1)}, u32[]{:S(2)}, u32[]{:S(2)}) %collective-permute-start.31) | collective-permute-done | bytes 262176 | tf_op jit(solution)/shard_map/ppermute | solution.py:26
  276.6 6.8 %collective-permute-done.33 = bf16[128,1024]{1,0:T(8,128)(2,1)S(1)} collective-permute-done((bf16[128,1024]{1,0:T(8,128)(2,1)S(1)}, bf16[128,1024]{1,0:T(8,128)(2,1)S(1)}, u32[]{:S(2)}, u32[]{:S(2)}) %collective-permute-start.33) | collective-permute-done | bytes 262176 | tf_op jit(solution)/shard_map/ppermute | solution.py:26
  306.7 6.6 %collective-permute-done.98 = bf16[2,4,16,1152]{3,2,0,1:T(8,128)(2,1)S(1)} collective-permute-done((bf16[2,4,16,1152]{3,2,0,1:T(8,128)(2,1)S(1)}, bf16[2,4,16,1152]{3,2,0,1:T(8,128)(2,1)S(1)}, u32[]{:S(2)}, u32[]{:S(2)}) %collective-permute-start.98) | collective-permute-done | bytes 294944 | tf_op jit(solution)/shard_map/ppermute | solution.py:22
  324.3 5.1 %collective-permute-done.103 = bf16[2,4,16,1152]{3,2,0,1:T(8,128)(2,1)S(1)} collective-permute-done((bf16[2,4,16,1152]{3,2,0,1:T(8,128)(2,1)S(1)}, bf16[2,4,16,1152]{3,2,0,1:T(8,128)(2,1)S(1)}, u32[]{:S(2)}, u32[]{:S(2)}) %collective-permute-start.103) | collective-permute-done | bytes 294944 | tf_op jit(solution)/shard_map/ppermute | solution.py:22
  343.2 5.5 %collective-permute-done.106 = bf16[2,16,1152]{2,1,0:T(8,128)(2,1)S(1)} collective-permute-done((bf16[2,16,1152]{2,1,0:T(8,128)(2,1)S(1)}, bf16[2,16,1152]{2,1,0:T(8,128)(2,1)S(1)}, u32[]{:S(2)}, u32[]{:S(2)}) %collective-permute-start.106) | collective-permute-done | bytes 73760 | tf_op jit(solution)/shard_map/ppermute | solution.py:22
  353.4 5.5 %collective-permute-done.108 = bf16[32,1152]{1,0:T(8,128)(2,1)S(1)} collective-permute-done((bf16[32,1152]{1,0:T(8,128)(2,1)S(1)}, bf16[32,1152]{1,0:T(8,128)(2,1)S(1)}, u32[]{:S(2)}, u32[]{:S(2)}) %collective-permute-start.108) | collective-permute-done | bytes 73760 | tf_op jit(solution)/shard_map/ppermute | solution.py:26
  377.1 5.4 %collective-permute-done.90 = bf16[2,4,16,2304]{3,2,0,1:T(8,128)(2,1)S(1)} collective-permute-done((bf16[2,4,16,2304]{3,2,0,1:T(8,128)(2,1)S(1)}, bf16[2,4,16,2304]{3,2,0,1:T(8,128)(2,1)S(1)}, u32[]{:S(2)}, u32[]{:S(2)}) %collective-permute-start.90) | collective-permute-done | bytes 589856 | tf_op jit(solution)/shard_map/ppermute | solution.py:22
  440.0 6.4 %collective-permute-start.75 = (bf16[2,16,1024]{2,1,0:T(8,128)(2,1)S(1)}, bf16[2,16,1024]{2,1,0:T(8,128)(2,1)S(1)}, u32[]{:S(2)}, u32[]{:S(2)}) collective-permute-start(bf16[2,16,1024]{2,1,0:T(8,128)(2,1)S(1)} %get-tuple-element.130), channel_id=1, source_target_pairs={{0,32},{16,48},{32,0},{48,16},{1,33},{17,49},{33,1},{49,17},{2,34}... | collective-permute-start | bytes 196616 | tf_op jit(solution)/shard_map/ppermute | solution.py:22
  452.3 4.4 collective-permute-start.80
  473.0 4.8 collective-permute-done.63
  (402 shorter events, 266.7 us)
Async XLA Ops:
  3.6 156.0 %collective-permute-start.1 = (bf16[128,1024]{1,0:T(8,128)(2,1)S(1)}, bf16[128,1024]{1,0:T(8,128)(2,1)S(1)}, u32[]{:S(2)}, u32[]{:S(2)}) collective-permute-start(bf16[128,1024]{1,0:T(8,128)(2,1)S(1)} %fusion.26), channel_id=1, source_target_pairs={{0,2},{2,0},{1,3},{3,1},{4,6},{6,4},{5,7},{7,5},{8,10},{10,8},{9,1... | collective-permute-start | bytes 786440 | tf_op jit(solution)/shard_map/ppermute | solution.py:26
  5.3 92.6 %collective-permute-start = (bf16[128,1024]{1,0:T(8,128)(2,1)S(1)}, bf16[128,1024]{1,0:T(8,128)(2,1)S(1)}, u32[]{:S(2)}, u32[]{:S(2)}) collective-permute-start(bf16[128,1024]{1,0:T(8,128)(2,1)S(1)} %fusion.26), channel_id=1, source_target_pairs={{0,1},{1,0},{2,3},{3,2},{4,5},{5,4},{6,7},{7,6},{8,9},{9,8},{10,11... | collective-permute-start | bytes 786440 | tf_op jit(solution)/shard_map/ppermute | solution.py:26
  5.3 157.7 %collective-permute-start.51 = (bf16[128,1024]{1,0:T(8,128)(2,1)}, bf16[128,1024]{1,0:T(8,128)(2,1)S(1)}, u32[]{:S(2)}, u32[]{:S(2)}) collective-permute-start(bf16[128,1024]{1,0:T(8,128)(2,1)} %param.21), channel_id=1, source_target_pairs={{0,2},{2,0},{1,3},{3,1},{4,6},{6,4},{5,7},{7,5},{8,10},{10,8},{9,1... | collective-permute-start | bytes 786440 | tf_op jit(solution)/shard_map/ppermute | solution.py:26
  5.7 95.2 %collective-permute-start.50 = (bf16[128,1024]{1,0:T(8,128)(2,1)}, bf16[128,1024]{1,0:T(8,128)(2,1)S(1)}, u32[]{:S(2)}, u32[]{:S(2)}) collective-permute-start(bf16[128,1024]{1,0:T(8,128)(2,1)} %param.21), channel_id=1, source_target_pairs={{0,1},{1,0},{2,3},{3,2},{4,5},{5,4},{6,7},{7,6},{8,9},{9,8},{10,11... | collective-permute-start | bytes 786440 | tf_op jit(solution)/shard_map/ppermute | solution.py:26
  6.7 14.2 %collective-permute-start.3 = (bf16[32,768]{1,0:T(8,128)(2,1)S(1)}, bf16[32,768]{1,0:T(8,128)(2,1)S(1)}, u32[]{:S(2)}, u32[]{:S(2)}) collective-permute-start(bf16[32,768]{1,0:T(8,128)(2,1)S(1)} %pad_maximum_fusion.35), channel_id=1, source_target_pairs={{0,64},{64,0},{1,65},{65,1},{2,66},{66,2},{3,67},{67,3},{4,68},{68... | collective-permute-start | bytes 147464 | tf_op jit(solution)/shard_map/ppermute | solution.py:26
  110.9 47.6 %collective-permute-start.45 = (bf16[2,4,16,1152]{3,2,1,0:T(8,128)(2,1)S(1)}, bf16[2,4,16,1152]{3,2,1,0:T(8,128)(2,1)S(1)}, u32[]{:S(2)}, u32[]{:S(2)}) collective-permute-start(bf16[2,4,16,1152]{3,2,1,0:T(8,128)(2,1)S(1)} %bitcast_dynamic-update-slice_fusion.32), channel_id=1, source_target_pairs={{0,16},{16,32},{32,48},{48,0},{1,17},{17,33},{33,49},{49,1},{2,18}... | collective-permute-start | bytes 884744 | tf_op jit(solution)/shard_map/ppermute | solution.py:22
  116.6 46.4 %collective-permute-start.46 = (bf16[2,4,16,1152]{3,2,1,0:T(8,128)(2,1)S(1)}, bf16[2,4,16,1152]{3,2,1,0:T(8,128)(2,1)S(1)}, u32[]{:S(2)}, u32[]{:S(2)}) collective-permute-start(bf16[2,4,16,1152]{3,2,1,0:T(8,128)(2,1)S(1)} %bitcast_dynamic-update-slice_fusion.32), channel_id=1, source_target_pairs={{0,48},{16,0},{32,16},{48,32},{1,49},{17,1},{33,17},{49,33},{2,50}... | collective-permute-start | bytes 884744 | tf_op jit(solution)/shard_map/ppermute | solution.py:22
  158.5 106.5 %collective-permute-start.39 = (bf16[2,4,16,1152]{3,2,1,0:T(8,128)(2,1)S(1)}, bf16[2,4,16,1152]{3,2,1,0:T(8,128)(2,1)S(1)}, u32[]{:S(2)}, u32[]{:S(2)}) collective-permute-start(bf16[2,4,16,1152]{3,2,1,0:T(8,128)(2,1)S(1)} %bitcast_dynamic-update-slice_fusion.36), channel_id=1, source_target_pairs={{0,4},{4,8},{8,12},{12,0},{1,5},{5,9},{9,13},{13,1},{2,6},{6,10},{... | collective-permute-start | bytes 884744 | tf_op jit(solution)/shard_map/ppermute | solution.py:22
  159.6 105.5 %collective-permute-start.40 = (bf16[2,4,16,1152]{3,2,1,0:T(8,128)(2,1)S(1)}, bf16[2,4,16,1152]{3,2,1,0:T(8,128)(2,1)S(1)}, u32[]{:S(2)}, u32[]{:S(2)}) collective-permute-start(bf16[2,4,16,1152]{3,2,1,0:T(8,128)(2,1)S(1)} %bitcast_dynamic-update-slice_fusion.36), channel_id=1, source_target_pairs={{0,12},{4,0},{8,4},{12,8},{1,13},{5,1},{9,5},{13,9},{2,14},{6,2},{... | collective-permute-start | bytes 884744 | tf_op jit(solution)/shard_map/ppermute | solution.py:22
  163.0 104.2 %collective-permute-start.41 = (bf16[2,4,16,1152]{3,2,1,0:T(8,128)(2,1)S(1)}, bf16[2,4,16,1152]{3,2,1,0:T(8,128)(2,1)S(1)}, u32[]{:S(2)}, u32[]{:S(2)}) collective-permute-start(bf16[2,4,16,1152]{3,2,1,0:T(8,128)(2,1)S(1)} %bitcast_dynamic-update-slice_fusion.36), channel_id=1, source_target_pairs={{0,8},{4,12},{8,0},{12,4},{1,9},{5,13},{9,1},{13,5},{2,10},{6,14},... | collective-permute-start | bytes 884744 | tf_op jit(solution)/shard_map/ppermute | solution.py:22
  164.6 111.9 %collective-permute-start.52 = (bf16[128,1024]{1,0:T(8,128)(2,1)S(1)}, bf16[128,1024]{1,0:T(8,128)(2,1)S(1)}, u32[]{:S(2)}, u32[]{:S(2)}) collective-permute-start(bf16[128,1024]{1,0:T(8,128)(2,1)S(1)} %collective-permute-done.51), channel_id=1, source_target_pairs={{0,1},{1,0},{2,3},{3,2},{4,5},{5,4},{6,7},{7,6},{8,9},{9,8},{10,11... | collective-permute-start | bytes 786440 | tf_op jit(solution)/shard_map/ppermute | solution.py:26
  171.6 19.2 %collective-permute-start.27 = (bf16[2,4,16,2560]{3,2,1,0:T(8,128)(2,1)S(1)}, bf16[2,4,16,2560]{3,2,1,0:T(8,128)(2,1)S(1)}, u32[]{:S(2)}, u32[]{:S(2)}) collective-permute-start(bf16[2,4,16,2560]{3,2,1,0:T(8,128)(2,1)S(1)} %bitcast_dynamic-update-slice_fusion.31), channel_id=1, source_target_pairs={{0,16},{16,32},{32,48},{48,0},{1,17},{17,33},{33,49},{49,1},{2,18}... | collective-permute-start | bytes 1966088 | tf_op jit(solution)/shard_map/ppermute | solution.py:22
  190.8 15.5 %collective-permute-start.28 = (bf16[2,4,16,2560]{3,2,1,0:T(8,128)(2,1)S(1)}, bf16[2,4,16,2560]{3,2,1,0:T(8,128)(2,1)S(1)}, u32[]{:S(2)}, u32[]{:S(2)}) collective-permute-start(bf16[2,4,16,2560]{3,2,1,0:T(8,128)(2,1)S(1)} %bitcast_dynamic-update-slice_fusion.31), channel_id=1, source_target_pairs={{0,48},{16,0},{32,16},{48,32},{1,49},{17,1},{33,17},{49,33},{2,50}... | collective-permute-start | bytes 1966088 | tf_op jit(solution)/shard_map/ppermute | solution.py:22
  206.3 16.1 %collective-permute-start.29 = (bf16[2,4,16,2560]{3,2,1,0:T(8,128)(2,1)S(1)}, bf16[2,4,16,2560]{3,2,1,0:T(8,128)(2,1)S(1)}, u32[]{:S(2)}, u32[]{:S(2)}) collective-permute-start(bf16[2,4,16,2560]{3,2,1,0:T(8,128)(2,1)S(1)} %bitcast_dynamic-update-slice_fusion.31), channel_id=1, source_target_pairs={{0,32},{16,48},{32,0},{48,16},{1,33},{17,49},{33,1},{49,17},{2,34}... | collective-permute-start | bytes 1966088 | tf_op jit(solution)/shard_map/ppermute | solution.py:22
  222.5 14.9 %collective-permute-start.21 = (bf16[2,4,16,2560]{3,2,1,0:T(8,128)(2,1)S(1)}, bf16[2,4,16,2560]{3,2,1,0:T(8,128)(2,1)S(1)}, u32[]{:S(2)}, u32[]{:S(2)}) collective-permute-start(bf16[2,4,16,2560]{3,2,1,0:T(8,128)(2,1)S(1)} %bitcast_dynamic-update-slice_fusion.27), channel_id=1, source_target_pairs={{0,4},{4,8},{8,12},{12,0},{1,5},{5,9},{9,13},{13,1},{2,6},{6,10},{... | collective-permute-start | bytes 1966088 | tf_op jit(solution)/shard_map/ppermute | solution.py:22
  237.4 14.3 %collective-permute-start.22 = (bf16[2,4,16,2560]{3,2,1,0:T(8,128)(2,1)S(1)}, bf16[2,4,16,2560]{3,2,1,0:T(8,128)(2,1)S(1)}, u32[]{:S(2)}, u32[]{:S(2)}) collective-permute-start(bf16[2,4,16,2560]{3,2,1,0:T(8,128)(2,1)S(1)} %bitcast_dynamic-update-slice_fusion.27), channel_id=1, source_target_pairs={{0,12},{4,0},{8,4},{12,8},{1,13},{5,1},{9,5},{13,9},{2,14},{6,2},{... | collective-permute-start | bytes 1966088 | tf_op jit(solution)/shard_map/ppermute | solution.py:22
  296.9 62.7 %collective-permute-start.53 = (bf16[2,128,1024]{2,1,0:T(8,128)(2,1)S(1)}, bf16[2,128,1024]{2,1,0:T(8,128)(2,1)S(1)}, u32[]{:S(2)}, u32[]{:S(2)}) collective-permute-start(bf16[2,128,1024]{2,1,0:T(8,128)(2,1)S(1)} %fusion.35), channel_id=1, source_target_pairs={{0,1},{1,0},{2,3},{3,2},{4,5},{5,4},{6,7},{7,6},{8,9},{9,8},{10,11... | collective-permute-start | bytes 1572872 | tf_op jit(solution)/shard_map/ppermute | solution.py:26
  300.3 62.3 %collective-permute-start.48 = (bf16[2,128,1024]{2,1,0:T(8,128)(2,1)S(1)}, bf16[2,128,1024]{2,1,0:T(8,128)(2,1)S(1)}, u32[]{:S(2)}, u32[]{:S(2)}) collective-permute-start(bf16[2,128,1024]{2,1,0:T(8,128)(2,1)S(1)} %fusion.33), channel_id=1, source_target_pairs={{0,1},{1,0},{2,3},{3,2},{4,5},{5,4},{6,7},{7,6},{8,9},{9,8},{10,11... | collective-permute-start | bytes 1572872 | tf_op jit(solution)/shard_map/ppermute | solution.py:26
  301.9 17.3 %collective-permute-start.97 = (bf16[2,4,16,1152]{3,2,0,1:T(8,128)(2,1)S(1)}, bf16[2,4,16,1152]{3,2,0,1:T(8,128)(2,1)S(1)}, u32[]{:S(2)}, u32[]{:S(2)}) collective-permute-start(bf16[2,4,16,1152]{3,2,0,1:T(8,128)(2,1)S(1)} %bitcast.505), channel_id=1, source_target_pairs={{0,12},{4,0},{8,4},{12,8},{1,13},{5,1},{9,5},{13,9},{2,14},{6,2},{... | collective-permute-start | bytes 884744 | tf_op jit(solution)/shard_map/ppermute | solution.py:22
  305.1 16.5 %collective-permute-start.96 = (bf16[2,4,16,1152]{3,2,0,1:T(8,128)(2,1)S(1)}, bf16[2,4,16,1152]{3,2,0,1:T(8,128)(2,1)S(1)}, u32[]{:S(2)}, u32[]{:S(2)}) collective-permute-start(bf16[2,4,16,1152]{3,2,0,1:T(8,128)(2,1)S(1)} %bitcast.504), channel_id=1, source_target_pairs={{0,4},{4,8},{8,12},{12,0},{1,5},{5,9},{9,13},{13,1},{2,6},{6,10},{... | collective-permute-start | bytes 884744 | tf_op jit(solution)/shard_map/ppermute | solution.py:22
  338.7 14.2 %collective-permute-start.105 = (bf16[2,16,1152]{2,1,0:T(8,128)(2,1)S(1)}, bf16[2,16,1152]{2,1,0:T(8,128)(2,1)S(1)}, u32[]{:S(2)}, u32[]{:S(2)}) collective-permute-start(bf16[2,16,1152]{2,1,0:T(8,128)(2,1)S(1)} %get-tuple-element.118), channel_id=1, source_target_pairs={{0,4},{4,8},{8,12},{12,0},{1,5},{5,9},{9,13},{13,1},{2,6},{6,10},{... | collective-permute-start | bytes 221192 | tf_op jit(solution)/shard_map/ppermute | solution.py:22
  339.6 25.1 %collective-permute-start.85 = (bf16[2,4,16,2304]{3,2,0,1:T(8,128)(2,1)S(1)}, bf16[2,4,16,2304]{3,2,0,1:T(8,128)(2,1)S(1)}, u32[]{:S(2)}, u32[]{:S(2)}) collective-permute-start(bf16[2,4,16,2304]{3,2,0,1:T(8,128)(2,1)S(1)} %bitcast.497), channel_id=1, source_target_pairs={{0,8},{4,12},{8,0},{12,4},{1,9},{5,13},{9,1},{13,5},{2,10},{6,14},... | collective-permute-start | bytes 1769480 | tf_op jit(solution)/shard_map/ppermute | solution.py:22
  348.7 17.2 %collective-permute-start.84 = (bf16[2,4,16,2304]{3,2,0,1:T(8,128)(2,1)S(1)}, bf16[2,4,16,2304]{3,2,0,1:T(8,128)(2,1)S(1)}, u32[]{:S(2)}, u32[]{:S(2)}) collective-permute-start(bf16[2,4,16,2304]{3,2,0,1:T(8,128)(2,1)S(1)} %bitcast.496), channel_id=1, source_target_pairs={{0,12},{4,0},{8,4},{12,8},{1,13},{5,1},{9,5},{13,9},{2,14},{6,2},{... | collective-permute-start | bytes 1769480 | tf_op jit(solution)/shard_map/ppermute | solution.py:22
  359.6 13.7 %collective-permute-start.91 = (bf16[2,4,16,2304]{3,2,0,1:T(8,128)(2,1)S(1)}, bf16[2,4,16,2304]{3,2,0,1:T(8,128)(2,1)S(1)}, u32[]{:S(2)}, u32[]{:S(2)}) collective-permute-start(bf16[2,4,16,2304]{3,2,0,1:T(8,128)(2,1)S(1)} %bitcast.500), channel_id=1, source_target_pairs={{0,32},{16,48},{32,0},{48,16},{1,33},{17,49},{33,1},{49,17},{2,34}... | collective-permute-start | bytes 1769480 | tf_op jit(solution)/shard_map/ppermute | solution.py:22
  362.6 19.9 %collective-permute-start.90 = (bf16[2,4,16,2304]{3,2,0,1:T(8,128)(2,1)S(1)}, bf16[2,4,16,2304]{3,2,0,1:T(8,128)(2,1)S(1)}, u32[]{:S(2)}, u32[]{:S(2)}) collective-permute-start(bf16[2,4,16,2304]{3,2,0,1:T(8,128)(2,1)S(1)} %bitcast.499), channel_id=1, source_target_pairs={{0,48},{16,0},{32,16},{48,32},{1,49},{17,1},{33,17},{49,33},{2,50}... | collective-permute-start | bytes 1769480 | tf_op jit(solution)/shard_map/ppermute | solution.py:22
  364.7 20.4 %collective-permute-start.89 = (bf16[2,4,16,2304]{3,2,0,1:T(8,128)(2,1)S(1)}, bf16[2,4,16,2304]{3,2,0,1:T(8,128)(2,1)S(1)}, u32[]{:S(2)}, u32[]{:S(2)}) collective-permute-start(bf16[2,4,16,2304]{3,2,0,1:T(8,128)(2,1)S(1)} %bitcast.498), channel_id=1, source_target_pairs={{0,16},{16,32},{32,48},{48,0},{1,17},{17,33},{33,49},{49,1},{2,18}... | collective-permute-start | bytes 1769480 | tf_op jit(solution)/shard_map/ppermute | solution.py:22
  365.9 34.2 %collective-permute-start.54 = (bf16[128,1024]{1,0:T(8,128)(2,1)S(1)}, bf16[128,1024]{1,0:T(8,128)(2,1)S(1)}, u32[]{:S(2)}, u32[]{:S(2)}) collective-permute-start(bf16[128,1024]{1,0:T(8,128)(2,1)S(1)} %fusion.59), channel_id=1, source_target_pairs={{0,2},{2,0},{1,3},{3,1},{4,6},{6,4},{5,7},{7,5},{8,10},{10,8},{9,1... | collective-permute-start | bytes 786440 | tf_op jit(solution)/shard_map/ppermute | solution.py:26
  370.0 30.5 %collective-permute-start.49 = (bf16[128,1024]{1,0:T(8,128)(2,1)S(1)}, bf16[128,1024]{1,0:T(8,128)(2,1)S(1)}, u32[]{:S(2)}, u32[]{:S(2)}) collective-permute-start(bf16[128,1024]{1,0:T(8,128)(2,1)S(1)} %fusion.58), channel_id=1, source_target_pairs={{0,2},{2,0},{1,3},{3,1},{4,6},{6,4},{5,7},{7,5},{8,10},{10,8},{9,1... | collective-permute-start | bytes 786440 | tf_op jit(solution)/shard_map/ppermute | solution.py:26
  425.4 14.3 %collective-permute-start.71 = (bf16[2,4,16,1024]{3,2,0,1:T(8,128)(2,1)S(1)}, bf16[2,4,16,1024]{3,2,0,1:T(8,128)(2,1)S(1)}, u32[]{:S(2)}, u32[]{:S(2)}) collective-permute-start(bf16[2,4,16,1024]{3,2,0,1:T(8,128)(2,1)S(1)} %bitcast.509), channel_id=1, source_target_pairs={{0,12},{4,0},{8,4},{12,8},{1,13},{5,1},{9,5},{13,9},{2,14},{6,2},{... | collective-permute-start | bytes 786440 | tf_op jit(solution)/shard_map/ppermute | solution.py:22
  430.2 26.5 %collective-permute-start.59 = (bf16[2,128,1024]{2,1,0:T(8,128)(2,1)S(1)}, bf16[2,128,1024]{2,1,0:T(8,128)(2,1)S(1)}, u32[]{:S(2)}, u32[]{:S(2)}) collective-permute-start(bf16[2,128,1024]{2,1,0:T(8,128)(2,1)S(1)} %fusion.36), channel_id=1, source_target_pairs={{0,1},{1,0},{2,3},{3,2},{4,5},{5,4},{6,7},{7,6},{8,9},{9,8},{10,11... | collective-permute-start | bytes 1572872 | tf_op jit(solution)/shard_map/ppermute | solution.py:26
  430.4 16.0 %collective-permute-start.78 = (bf16[2,4,16,1024]{3,2,1,0:T(8,128)(2,1)S(1)}, bf16[2,4,16,1024]{3,2,1,0:T(8,128)(2,1)S(1)}, u32[]{:S(2)}, u32[]{:S(2)}) collective-permute-start(bf16[2,4,16,1024]{3,2,1,0:T(8,128)(2,1)S(1)} %get-tuple-element.75), channel_id=1, source_target_pairs={{0,32},{16,48},{32,0},{48,16},{1,33},{17,49},{33,1},{49,17},{2,34}... | collective-permute-start | bytes 786440 | tf_op jit(solution)/shard_map/ppermute | solution.py:22
  434.7 14.2 %collective-permute-start.77 = (bf16[2,4,16,1024]{3,2,1,0:T(8,128)(2,1)S(1)}, bf16[2,4,16,1024]{3,2,1,0:T(8,128)(2,1)S(1)}, u32[]{:S(2)}, u32[]{:S(2)}) collective-permute-start(bf16[2,4,16,1024]{3,2,1,0:T(8,128)(2,1)S(1)} %get-tuple-element.76), channel_id=1, source_target_pairs={{0,48},{16,0},{32,16},{48,32},{1,49},{17,1},{33,17},{49,33},{2,50}... | collective-permute-start | bytes 786440 | tf_op jit(solution)/shard_map/ppermute | solution.py:22
  (84 other events, 658.0 us)
